TPU v7x, 512 devices: a whole 4x8x8 slice. The times are simulated.
512 devices in a mesh: row: 16 (over y, z_hi), col: 32 (over x, z_lo, core).
Axes of the slice: x: 4, y: 8, z: 8 (z_hi: 2, z_lo: 4; z = z_hi * 4 + z_lo), core: 2. Of those that a mesh axis runs over, the one named last changes fastest.
Arguments:
- factor: bfloat16 [28672, 28672], P('row', 'col'), may hold values from -2 to 2, as said below
- gradient: float32 [28672, 2048], P(('row', 'col')), may hold values from -6 to 6
- starts: int32 [16], replicated, may hold values from 0 to 15, each once
Outputs:
- solved: float32 [28672, 2048], P(('row', 'col'))
Inputs may be any that keep to these rules, and one draw needn't show every extreme that they name: `factor`: tiles above the block diagonal are zero, and every diagonal tile is upper triangular. `starts`: every block column is the start of exactly one panel.
All inputs are finite; a program needn't handle non-finite values.
Results may differ from a plain program's by a relative error of at most 0.0046.
Values may be sent and summed in bfloat16 or wider, within the bound.
A program may use at most 64 MiB of HBM per device.

v0:
```python
import jax
import jax.numpy as jnp
from jax import lax
from jax.sharding import PartitionSpec as P

TICKS = 6


def partner(array, axis, bit):
    return lax.ppermute(array, axis, [(i, i ^ 1 << bit) for i in range(lax.axis_size(axis))])


def broadcast(value, axis, source):
    kept = jnp.where(lax.axis_index(axis) == source, value, 0).astype(value.dtype)
    return lax.psum(kept, axis)


def shifted(block, axis, distance):
    devices = range(lax.axis_size(axis))
    route = [((i - distance) % len(devices), i) for i in devices]
    return lax.ppermute(block, axis, route)


def body(factor, gradient, starts):
    row_count = gradient.shape[0]
    block_count = starts.shape[0]
    panel_width = gradient.shape[1] // block_count
    tile_rows = factor.shape[0]
    half_rows = factor.shape[1]
    col_count = lax.axis_size("col")
    row_idx = lax.axis_index("row")
    col_idx = lax.axis_index("col")
    block_col = col_idx // 2
    half_idx = col_idx % 2
    slots = jnp.arange(block_count, dtype=jnp.int32)
    start_hot = (starts[None, :] == slots[:, None]).astype(jnp.float32)
    pieces = gradient.reshape(2, row_count // 2, block_count, panel_width)
    ordered = jnp.einsum("jp,hrpw->jhrw", start_hot, pieces, precision=lax.Precision.HIGHEST)
    ordered = ordered.reshape(col_count * (row_count // 2), panel_width)
    received = lax.all_to_all(ordered, "col", split_axis=0, concat_axis=0, tiled=True)
    received = received.reshape(col_count, row_count // 2, panel_width)
    keep_first = (half_idx == 0).astype(jnp.float32)
    keep_second = 1.0 - keep_first
    buffer = jnp.stack([received * keep_first, received * keep_second], axis=1).reshape(
        tile_rows, panel_width
    )
    zeros_tile = jnp.zeros((tile_rows, panel_width), jnp.float32)
    for tick_idx in range(TICKS):
        active = block_col >= tick_idx
        on_diag = active & (row_idx == block_col)
        below_diag = active & (row_idx > block_col)
        summed = buffer + partner(buffer, "col", 0)
        rounded = summed.astype(jnp.bfloat16)
        solution = lax.dot_general(
            factor, rounded, (((0,), (0,)), ((), ())), preferred_element_type=jnp.float32
        )
        solution_bf = solution.astype(jnp.bfloat16)
        arrived = broadcast(solution_bf, "row", block_col)
        update = jnp.dot(factor, arrived, preferred_element_type=jnp.float32)
        placed = lax.dynamic_update_slice_in_dim(zeros_tile, solution, half_idx * half_rows, 0)
        buffer = jnp.where(on_diag, placed, jnp.where(below_diag, buffer - update, buffer))
        if tick_idx + 1 < TICKS:
            buffer = shifted(buffer, "col", 2)
    end_hot = (((starts + (TICKS - 1)) % block_count)[None, :] == slots[:, None]).astype(
        jnp.float32
    )
    returned = lax.all_to_all(buffer, "col", split_axis=0, concat_axis=0, tiled=True)
    slot_rows = returned.reshape(block_count, 2, row_count, panel_width).sum(axis=1)
    result = jnp.einsum("jp,jrw->rpw", end_hot, slot_rows, precision=lax.Precision.HIGHEST)
    return result.reshape(row_count, block_count * panel_width)


def solution(mesh):
    in_specs = (P("row", "col"), P(("row", "col"), None), P())
    out_specs = P(("row", "col"), None)
    return jax.shard_map(body, mesh=mesh, in_specs=in_specs, out_specs=out_specs, check_vma=False)
```

profile of v0, /device:TPU:1, one launch (start us, length us, event | category | flops | bytes accessed | tf_op | source)
XLA Modules:
  0.0 1403.5 jit_solution(1890911971000149336)
XLA Ops:
  10.2 11.3 all-to-all-start
  21.6 16.8 %all-to-all-done = f32[32,28,128]{2,1,0:T(8,128)} async-done(((f32[32,28,128]{2,1,0:T(8,128)}), f32[32,28,128]{2,1,0:T(8,128)}, u32[]{:S(2)}, u32[]{:S(2)}) %all-to-all-start) | async-done | bytes 458784 | tf_op jit(solution)/shard_map/all_to_all | solution.py:40
  45.1 2.6 collective-permute-done
  48.7 2.9 constant_dynamic-update-slice_fusion.5
  54.9 185.7 %all-reduce.7.cloned.1.call-done = bf16[896,128]{0,1:T(8,128)(2,1)} async-done(((bf16[896,128]{0,1:T(8,128)(2,1)}), bf16[896,128]{0,1:T(8,128)(2,1)}) %all-reduce.7.cloned.1.call-update) | async-done | bytes 229392 | tf_op jit(solution)/shard_map/psum | solution.py:15
  240.6 2.6 fusion.17
  245.4 15.9 %collective-permute-done.1 = f32[1792,128]{0,1:T(8,128)S(1)} collective-permute-done((f32[1792,128]{0,1:T(8,128)S(1)}, f32[1792,128]{0,1:T(8,128)S(1)}, u32[]{:S(2)}, u32[]{:S(2)}) %collective-permute-start.1) | collective-permute-done | bytes 917536 | tf_op jit(solution)/shard_map/ppermute | solution.py:21
  261.3 14.7 %collective-permute-start.2 = (f32[1792,128]{0,1:T(8,128)S(1)}, f32[1792,128]{0,1:T(8,128)S(1)}, u32[]{:S(2)}, u32[]{:S(2)}) collective-permute-start(f32[1792,128]{0,1:T(8,128)S(1)} %collective-permute-done.1), channel_id=1, source_target_pairs={{0,1},{1,0},{2,3},{3,2},{4,5},{5,4},{6,7},{7,6},{8,9},{9,8},{10,11... | collective-permute-start | bytes 2752520 | tf_op jit(solution)/shard_map/ppermute | solution.py:10
  281.4 180.4 %all-reduce.9.cloned.1.call-done = bf16[896,128]{0,1:T(8,128)(2,1)} async-done(((bf16[896,128]{0,1:T(8,128)(2,1)}), bf16[896,128]{0,1:T(8,128)(2,1)}) %all-reduce.9.cloned.1.call-update) | async-done | bytes 229392 | tf_op jit(solution)/shard_map/psum | solution.py:15
  466.5 15.6 %collective-permute-done.3 = f32[1792,128]{0,1:T(8,128)S(1)} collective-permute-done((f32[1792,128]{0,1:T(8,128)S(1)}, f32[1792,128]{0,1:T(8,128)S(1)}, u32[]{:S(2)}, u32[]{:S(2)}) %collective-permute-start.3) | collective-permute-done | bytes 917536 | tf_op jit(solution)/shard_map/ppermute | solution.py:21
  482.2 14.7 %collective-permute-start.4 = (f32[1792,128]{0,1:T(8,128)S(1)}, f32[1792,128]{0,1:T(8,128)S(1)}, u32[]{:S(2)}, u32[]{:S(2)}) collective-permute-start(f32[1792,128]{0,1:T(8,128)S(1)} %collective-permute-done.3), channel_id=1, source_target_pairs={{0,1},{1,0},{2,3},{3,2},{4,5},{5,4},{6,7},{7,6},{8,9},{9,8},{10,11... | collective-permute-start | bytes 2752520 | tf_op jit(solution)/shard_map/ppermute | solution.py:10
  502.3 180.6 %all-reduce.11.cloned.1.call-done = bf16[896,128]{0,1:T(8,128)(2,1)} async-done(((bf16[896,128]{0,1:T(8,128)(2,1)}), bf16[896,128]{0,1:T(8,128)(2,1)}) %all-reduce.11.cloned.1.call-update) | async-done | bytes 229392 | tf_op jit(solution)/shard_map/psum | solution.py:15
  687.7 15.6 %collective-permute-done.5 = f32[1792,128]{0,1:T(8,128)S(1)} collective-permute-done((f32[1792,128]{0,1:T(8,128)S(1)}, f32[1792,128]{0,1:T(8,128)S(1)}, u32[]{:S(2)}, u32[]{:S(2)}) %collective-permute-start.5) | collective-permute-done | bytes 917536 | tf_op jit(solution)/shard_map/ppermute | solution.py:21
  703.3 14.7 %collective-permute-start.6 = (f32[1792,128]{0,1:T(8,128)S(1)}, f32[1792,128]{0,1:T(8,128)S(1)}, u32[]{:S(2)}, u32[]{:S(2)}) collective-permute-start(f32[1792,128]{0,1:T(8,128)S(1)} %collective-permute-done.5), channel_id=1, source_target_pairs={{0,1},{1,0},{2,3},{3,2},{4,5},{5,4},{6,7},{7,6},{8,9},{9,8},{10,11... | collective-permute-start | bytes 2752520 | tf_op jit(solution)/shard_map/ppermute | solution.py:10
  723.4 180.7 %all-reduce.13.cloned.1.call-done = bf16[896,128]{0,1:T(8,128)(2,1)} async-done(((bf16[896,128]{0,1:T(8,128)(2,1)}), bf16[896,128]{0,1:T(8,128)(2,1)}) %all-reduce.13.cloned.1.call-update) | async-done | bytes 229392 | tf_op jit(solution)/shard_map/psum | solution.py:15
  908.9 15.6 %collective-permute-done.7 = f32[1792,128]{0,1:T(8,128)S(1)} collective-permute-done((f32[1792,128]{0,1:T(8,128)S(1)}, f32[1792,128]{0,1:T(8,128)S(1)}, u32[]{:S(2)}, u32[]{:S(2)}) %collective-permute-start.7) | collective-permute-done | bytes 917536 | tf_op jit(solution)/shard_map/ppermute | solution.py:21
  924.5 14.7 %collective-permute-start.8 = (f32[1792,128]{0,1:T(8,128)S(1)}, f32[1792,128]{0,1:T(8,128)S(1)}, u32[]{:S(2)}, u32[]{:S(2)}) collective-permute-start(f32[1792,128]{0,1:T(8,128)S(1)} %collective-permute-done.7), channel_id=1, source_target_pairs={{0,1},{1,0},{2,3},{3,2},{4,5},{5,4},{6,7},{7,6},{8,9},{9,8},{10,11... | collective-permute-start | bytes 2752520 | tf_op jit(solution)/shard_map/ppermute | solution.py:10
  944.6 180.7 %all-reduce.15.cloned.1.call-done = bf16[896,128]{0,1:T(8,128)(2,1)} async-done(((bf16[896,128]{0,1:T(8,128)(2,1)}), bf16[896,128]{0,1:T(8,128)(2,1)}) %all-reduce.15.cloned.1.call-update) | async-done | bytes 229392 | tf_op jit(solution)/shard_map/psum | solution.py:15
  1130.2 15.6 %collective-permute-done.9 = f32[1792,128]{0,1:T(8,128)S(1)} collective-permute-done((f32[1792,128]{0,1:T(8,128)S(1)}, f32[1792,128]{0,1:T(8,128)S(1)}, u32[]{:S(2)}, u32[]{:S(2)}) %collective-permute-start.9) | collective-permute-done | bytes 917536 | tf_op jit(solution)/shard_map/ppermute | solution.py:21
  1145.8 14.9 %collective-permute-start.10 = (f32[1792,128]{0,1:T(8,128)S(1)}, f32[1792,128]{0,1:T(8,128)S(1)}, u32[]{:S(2)}, u32[]{:S(2)}) collective-permute-start(f32[1792,128]{0,1:T(8,128)S(1)} %collective-permute-done.9), channel_id=1, source_target_pairs={{0,1},{1,0},{2,3},{3,2},{4,5},{5,4},{6,7},{7,6},{8,9},{9,8},{10,11... | collective-permute-start | bytes 2752520 | tf_op jit(solution)/shard_map/ppermute | solution.py:10
  1165.8 180.7 %all-reduce.17.cloned.1.call-done = bf16[896,128]{0,1:T(8,128)(2,1)} async-done(((bf16[896,128]{0,1:T(8,128)(2,1)}), bf16[896,128]{0,1:T(8,128)(2,1)}) %all-reduce.17.cloned.1.call-update) | async-done | bytes 229392 | tf_op jit(solution)/shard_map/psum | solution.py:15
  1346.6 3.3 fusion.2
  1352.3 16.6 %all-to-all-start.1 = ((f32[32,56,128]{2,1,0:T(8,128)}), f32[32,56,128]{2,1,0:T(8,128)}, u32[]{:S(2)}, u32[]{:S(2)}) async-start(f32[32,56,128]{2,1,0:T(8,128)} %bitcast.103), calls=%async_computation.1 | async-start | bytes 1835008 | tf_op jit(solution)/shard_map/all_to_all | solution.py:67
  1369.0 25.1 %all-to-all-done.1 = f32[32,56,128]{2,1,0:T(8,128)} async-done(((f32[32,56,128]{2,1,0:T(8,128)}), f32[32,56,128]{2,1,0:T(8,128)}, u32[]{:S(2)}, u32[]{:S(2)}) %all-to-all-start.1) | async-done | bytes 917536 | tf_op jit(solution)/shard_map/all_to_all | solution.py:67
  (72 shorter events, 67.6 us)
Async XLA Ops:
  6.5 42.2 %copy-start = (bf16[1792,896]{1,0:T(8,128)(2,1)S(1)}, bf16[1792,896]{1,0:T(8,128)(2,1)}, u32[]{:S(2)}) copy-start(bf16[1792,896]{1,0:T(8,128)(2,1)} %param.3) | copy-start | bytes 9633796
  10.2 28.2 %all-to-all-start = ((f32[32,28,128]{2,1,0:T(8,128)}), f32[32,28,128]{2,1,0:T(8,128)}, u32[]{:S(2)}, u32[]{:S(2)}) async-start(f32[32,28,128]{2,1,0:T(8,128)} %copy.11), calls=%async_computation | async-start | bytes 1048576 | tf_op jit(solution)/shard_map/all_to_all | solution.py:40
  21.5 219.0 %all-reduce.7.cloned.1.call-start = ((), (), s32[]{:S(2)}) async-start(), calls=%async_computation.2 | async-start | bytes 458752 | tf_op jit(solution)/shard_map/psum | solution.py:15
  43.0 4.7 collective-permute-start
  52.4 409.4 %all-reduce.9.cloned.1.call-start = ((), (), s32[]{:S(2)}) async-start(), calls=%async_computation.3 | async-start | bytes 458752 | tf_op jit(solution)/shard_map/psum | solution.py:15
  243.2 18.1 %collective-permute-start.1 = (f32[1792,128]{0,1:T(8,128)S(1)}, f32[1792,128]{0,1:T(8,128)S(1)}, u32[]{:S(2)}, u32[]{:S(2)}) collective-permute-start(f32[1792,128]{0,1:T(8,128)S(1)} %fusion.17), channel_id=1, source_target_pairs={{30,0},{31,1},{0,2},{1,3},{2,4},{3,5},{4,6},{5,7},{6,8},{7,9},{8,1... | collective-permute-start | bytes 2752520 | tf_op jit(solution)/shard_map/ppermute | solution.py:21
  261.3 19.3 %copy-start.2 = (f32[1792,128]{0,1:T(8,128)}, f32[1792,128]{0,1:T(8,128)S(1)}, u32[]{:S(2)}) copy-start(f32[1792,128]{0,1:T(8,128)S(1)} %collective-permute-done.1) | copy-start | bytes 2752516
  261.3 16.8 %collective-permute-start.2 = (f32[1792,128]{0,1:T(8,128)S(1)}, f32[1792,128]{0,1:T(8,128)S(1)}, u32[]{:S(2)}, u32[]{:S(2)}) collective-permute-start(f32[1792,128]{0,1:T(8,128)S(1)} %collective-permute-done.1), channel_id=1, source_target_pairs={{0,1},{1,0},{2,3},{3,2},{4,5},{5,4},{6,7},{7,6},{8,9},{9,8},{10,11... | collective-permute-start | bytes 2752520 | tf_op jit(solution)/shard_map/ppermute | solution.py:10
  281.3 401.6 %all-reduce.11.cloned.1.call-start = ((), (), s32[]{:S(2)}) async-start(), calls=%async_computation.4 | async-start | bytes 458752 | tf_op jit(solution)/shard_map/psum | solution.py:15
  464.1 18.1 %collective-permute-start.3 = (f32[1792,128]{0,1:T(8,128)S(1)}, f32[1792,128]{0,1:T(8,128)S(1)}, u32[]{:S(2)}, u32[]{:S(2)}) collective-permute-start(f32[1792,128]{0,1:T(8,128)S(1)} %fusion.14), channel_id=1, source_target_pairs={{30,0},{31,1},{0,2},{1,3},{2,4},{3,5},{4,6},{5,7},{6,8},{7,9},{8,1... | collective-permute-start | bytes 2752520 | tf_op jit(solution)/shard_map/ppermute | solution.py:21
  482.2 19.3 %copy-start.3 = (f32[1792,128]{0,1:T(8,128)}, f32[1792,128]{0,1:T(8,128)S(1)}, u32[]{:S(2)}) copy-start(f32[1792,128]{0,1:T(8,128)S(1)} %collective-permute-done.3) | copy-start | bytes 2752516
  482.2 16.8 %collective-permute-start.4 = (f32[1792,128]{0,1:T(8,128)S(1)}, f32[1792,128]{0,1:T(8,128)S(1)}, u32[]{:S(2)}, u32[]{:S(2)}) collective-permute-start(f32[1792,128]{0,1:T(8,128)S(1)} %collective-permute-done.3), channel_id=1, source_target_pairs={{0,1},{1,0},{2,3},{3,2},{4,5},{5,4},{6,7},{7,6},{8,9},{9,8},{10,11... | collective-permute-start | bytes 2752520 | tf_op jit(solution)/shard_map/ppermute | solution.py:10
  502.2 401.9 %all-reduce.13.cloned.1.call-start = ((), (), s32[]{:S(2)}) async-start(), calls=%async_computation.5 | async-start | bytes 458752 | tf_op jit(solution)/shard_map/psum | solution.py:15
  685.2 18.1 %collective-permute-start.5 = (f32[1792,128]{0,1:T(8,128)S(1)}, f32[1792,128]{0,1:T(8,128)S(1)}, u32[]{:S(2)}, u32[]{:S(2)}) collective-permute-start(f32[1792,128]{0,1:T(8,128)S(1)} %fusion.11), channel_id=1, source_target_pairs={{30,0},{31,1},{0,2},{1,3},{2,4},{3,5},{4,6},{5,7},{6,8},{7,9},{8,1... | collective-permute-start | bytes 2752520 | tf_op jit(solution)/shard_map/ppermute | solution.py:21
  703.3 19.3 %copy-start.4 = (f32[1792,128]{0,1:T(8,128)}, f32[1792,128]{0,1:T(8,128)S(1)}, u32[]{:S(2)}) copy-start(f32[1792,128]{0,1:T(8,128)S(1)} %collective-permute-done.5) | copy-start | bytes 2752516
  703.3 16.8 %collective-permute-start.6 = (f32[1792,128]{0,1:T(8,128)S(1)}, f32[1792,128]{0,1:T(8,128)S(1)}, u32[]{:S(2)}, u32[]{:S(2)}) collective-permute-start(f32[1792,128]{0,1:T(8,128)S(1)} %collective-permute-done.5), channel_id=1, source_target_pairs={{0,1},{1,0},{2,3},{3,2},{4,5},{5,4},{6,7},{7,6},{8,9},{9,8},{10,11... | collective-permute-start | bytes 2752520 | tf_op jit(solution)/shard_map/ppermute | solution.py:10
  723.4 402.0 %all-reduce.15.cloned.1.call-start = ((), (), s32[]{:S(2)}) async-start(), calls=%async_computation.6 | async-start | bytes 458752 | tf_op jit(solution)/shard_map/psum | solution.py:15
  906.4 18.1 %collective-permute-start.7 = (f32[1792,128]{0,1:T(8,128)S(1)}, f32[1792,128]{0,1:T(8,128)S(1)}, u32[]{:S(2)}, u32[]{:S(2)}) collective-permute-start(f32[1792,128]{0,1:T(8,128)S(1)} %fusion.8), channel_id=1, source_target_pairs={{30,0},{31,1},{0,2},{1,3},{2,4},{3,5},{4,6},{5,7},{6,8},{7,9},{8,1... | collective-permute-start | bytes 2752520 | tf_op jit(solution)/shard_map/ppermute | solution.py:21
  924.5 19.3 %copy-start.5 = (f32[1792,128]{0,1:T(8,128)}, f32[1792,128]{0,1:T(8,128)S(1)}, u32[]{:S(2)}) copy-start(f32[1792,128]{0,1:T(8,128)S(1)} %collective-permute-done.7) | copy-start | bytes 2752516
  924.5 16.8 %collective-permute-start.8 = (f32[1792,128]{0,1:T(8,128)S(1)}, f32[1792,128]{0,1:T(8,128)S(1)}, u32[]{:S(2)}, u32[]{:S(2)}) collective-permute-start(f32[1792,128]{0,1:T(8,128)S(1)} %collective-permute-done.7), channel_id=1, source_target_pairs={{0,1},{1,0},{2,3},{3,2},{4,5},{5,4},{6,7},{7,6},{8,9},{9,8},{10,11... | collective-permute-start | bytes 2752520 | tf_op jit(solution)/shard_map/ppermute | solution.py:10
  944.6 402.0 %all-reduce.17.cloned.1.call-start = ((), (), s32[]{:S(2)}) async-start(), calls=%async_computation.7 | async-start | bytes 458752 | tf_op jit(solution)/shard_map/psum | solution.py:15
  1127.7 18.1 %collective-permute-start.9 = (f32[1792,128]{0,1:T(8,128)S(1)}, f32[1792,128]{0,1:T(8,128)S(1)}, u32[]{:S(2)}, u32[]{:S(2)}) collective-permute-start(f32[1792,128]{0,1:T(8,128)S(1)} %fusion.5), channel_id=1, source_target_pairs={{30,0},{31,1},{0,2},{1,3},{2,4},{3,5},{4,6},{5,7},{6,8},{7,9},{8,1... | collective-permute-start | bytes 2752520 | tf_op jit(solution)/shard_map/ppermute | solution.py:21
  1145.8 16.8 %collective-permute-start.10 = (f32[1792,128]{0,1:T(8,128)S(1)}, f32[1792,128]{0,1:T(8,128)S(1)}, u32[]{:S(2)}, u32[]{:S(2)}) collective-permute-start(f32[1792,128]{0,1:T(8,128)S(1)} %collective-permute-done.9), channel_id=1, source_target_pairs={{0,1},{1,0},{2,3},{3,2},{4,5},{5,4},{6,7},{7,6},{8,9},{9,8},{10,11... | collective-permute-start | bytes 2752520 | tf_op jit(solution)/shard_map/ppermute | solution.py:10
  1352.3 41.8 %all-to-all-start.1 = ((f32[32,56,128]{2,1,0:T(8,128)}), f32[32,56,128]{2,1,0:T(8,128)}, u32[]{:S(2)}, u32[]{:S(2)}) async-start(f32[32,56,128]{2,1,0:T(8,128)} %bitcast.103), calls=%async_computation.1 | async-start | bytes 1835008 | tf_op jit(solution)/shard_map/all_to_all | solution.py:67
  (2 other events, 38.4 us)
Sparse Core Ops, SparseCore 0:
  52.5 188.0 all-reduce.6
  281.4 180.2 all-reduce.8
  502.3 180.5 all-reduce.10
  723.5 180.5 all-reduce.12
  944.7 180.6 all-reduce.14
  1165.9 180.5 all-reduce.16
where the time goes:
time: 1400 us
  waiting for transfers between devices  1220 us (87%)
  starting transfers between devices  116 us (8%)
  matrix products  27.1 us (2%)
  local copies, waits for them, and re-layouts  17.9 us (1%)
    psum x6, waiting for transfers between devices, broadcast(): return lax.psum(kept, axis)  1090 us
    ppermute x5, waiting for transfers between devices, shifted(): return lax.ppermute(block, axis, route)  78.4 us
    ppermute x6, starting transfers between devices, partner(): lax.ppermute(array, axis, [(i, i ^ 1 << bit) for i in range(lax.axis_size...  75.6 us
  transfers between devices with their start and end apart: 19, of which 19 were waited for; matrix products, arithmetic and copies ran while one was open for 0% of the time, Pallas kernels for 0%

commit v1 on v0

--- a/solution.py
+++ b/solution.py
@@ -12,7 +12,7 @@
 
 def broadcast(value, axis, source):
     kept = jnp.where(lax.axis_index(axis) == source, value, 0).astype(value.dtype)
-    return lax.psum(kept, axis)
+    return jnp.sum(lax.all_gather(kept, axis), axis=0)
 
 
 def shifted(block, axis, distance):

time: 1400 us -> 1020 us (0.73)
  waiting for transfers between devices: 1220 us -> 867 us
  starting transfers between devices: 116 us -> 65.9 us
  local copies, waits for them, and re-layouts: 17.9 us -> 34.2 us
    psum x6 -> x0, waiting for transfers between devices: 1090 us -> none  [broadcast(): return lax.psum(kept, axis)]
    all_gather x0 -> x6, waiting for transfers between devices: none -> 703 us  [broadcast(): return jnp.sum(lax.all_gather(kept, axis), axis=0)]
    ppermute x6, starting transfers between devices: 75.6 us -> 35.2 us  [partner(): lax.ppermute(array, axis, [(i, i ^ 1 << bit) for i in range(lax.axis_size...]
    ppermute x5, waiting for transfers between devices: 78.4 us -> 110 us  [shifted(): return lax.ppermute(block, axis, route)]
    unnamed x16 -> x34, local copies, waits for them, and re-layouts: 2.19 us -> 18.5 us
where the time goes in v1:
time: 1020 us
  waiting for transfers between devices  867 us (85%)
  starting transfers between devices  65.9 us (6%)
  local copies, waits for them, and re-layouts  34.2 us (3%)
  matrix products  20 us (2%)
  other arithmetic  17.4 us (2%)
  between operations  14 us (1%)
    all_gather x6, waiting for transfers between devices, broadcast(): return jnp.sum(lax.all_gather(kept, axis), axis=0)  703 us
    ppermute x5, waiting for transfers between devices, shifted(): return lax.ppermute(block, axis, route)  110 us
    ppermute x6, starting transfers between devices, partner(): lax.ppermute(array, axis, [(i, i ^ 1 << bit) for i in range(lax.axis_size...  35.2 us
    all_to_all x1, waiting for transfers between devices, body(): lax.all_to_all(buffer, 'col', split_axis=0, concat_axis=0, tiled=True)  25.1 us
  transfers between devices with their start and end apart: 19, of which 19 were waited for; matrix products, arithmetic and copies ran while one was open for 0% of the time, Pallas kernels for 0%

profile of v1, /device:TPU:1, one launch (start us, length us, event | category | flops | bytes accessed | tf_op | source)
XLA Modules:
  0.0 1018.6 jit_solution(7055214598382885685)
XLA Ops:
  10.2 11.3 %all-to-all-start = ((f32[32,28,128]{2,1,0:T(8,128)}), f32[32,28,128]{2,1,0:T(8,128)}, u32[]{:S(2)}, u32[]{:S(2)}) async-start(f32[32,28,128]{2,1,0:T(8,128)} %copy.11), calls=%async_computation | async-start | bytes 1048576 | tf_op jit(solution)/shard_map/all_to_all | solution.py:40
  21.6 16.8 %all-to-all-done = f32[32,28,128]{2,1,0:T(8,128)} async-done(((f32[32,28,128]{2,1,0:T(8,128)}), f32[32,28,128]{2,1,0:T(8,128)}, u32[]{:S(2)}, u32[]{:S(2)}) %all-to-all-start) | async-done | bytes 458784 | tf_op jit(solution)/shard_map/all_to_all | solution.py:40
  48.7 2.9 constant_dynamic-update-slice_fusion.5
  54.8 120.5 %all-gather.13.cloned.1.call-done = bf16[14336,128]{0,1:T(8,128)(2,1)} async-done(((bf16[896,128]{0,1:T(8,128)(2,1)}), bf16[14336,128]{0,1:T(8,128)(2,1)}) %all-gather.13.cloned.1.call-update) | async-done | bytes 3670032 | tf_op jit(solution)/shard_map/all_gather | solution.py:15
  184.0 21.9 %collective-permute-done.1 = f32[1792,128]{0,1:T(8,128)S(1)} collective-permute-done((f32[1792,128]{0,1:T(8,128)S(1)}, f32[1792,128]{0,1:T(8,128)S(1)}, u32[]{:S(2)}, u32[]{:S(2)}) %collective-permute-start.1) | collective-permute-done | bytes 917536 | tf_op jit(solution)/shard_map/ppermute | solution.py:21
  206.0 6.6 collective-permute-start.2
  217.9 115.5 %all-gather.15.cloned.1.call-done = bf16[14336,128]{0,1:T(8,128)(2,1)} async-done(((bf16[896,128]{0,1:T(8,128)(2,1)}), bf16[14336,128]{0,1:T(8,128)(2,1)}) %all-gather.15.cloned.1.call-update) | async-done | bytes 3670032 | tf_op jit(solution)/shard_map/all_gather | solution.py:15
  340.9 21.9 %collective-permute-done.3 = f32[1792,128]{0,1:T(8,128)S(1)} collective-permute-done((f32[1792,128]{0,1:T(8,128)S(1)}, f32[1792,128]{0,1:T(8,128)S(1)}, u32[]{:S(2)}, u32[]{:S(2)}) %collective-permute-start.3) | collective-permute-done | bytes 917536 | tf_op jit(solution)/shard_map/ppermute | solution.py:21
  362.9 6.6 collective-permute-start.4
  375.0 116.5 %all-gather.17.cloned.1.call-done = bf16[14336,128]{0,1:T(8,128)(2,1)} async-done(((bf16[896,128]{0,1:T(8,128)(2,1)}), bf16[14336,128]{0,1:T(8,128)(2,1)}) %all-gather.17.cloned.1.call-update) | async-done | bytes 3670032 | tf_op jit(solution)/shard_map/all_gather | solution.py:15
  491.5 2.7 copy.21
  499.0 21.9 %collective-permute-done.5 = f32[1792,128]{0,1:T(8,128)S(1)} collective-permute-done((f32[1792,128]{0,1:T(8,128)S(1)}, f32[1792,128]{0,1:T(8,128)S(1)}, u32[]{:S(2)}, u32[]{:S(2)}) %collective-permute-start.5) | collective-permute-done | bytes 917536 | tf_op jit(solution)/shard_map/ppermute | solution.py:21
  520.9 6.6 collective-permute-start.6
  532.9 116.7 %all-gather.19.cloned.1.call-done = bf16[14336,128]{0,1:T(8,128)(2,1)} async-done(((bf16[896,128]{0,1:T(8,128)(2,1)}), bf16[14336,128]{0,1:T(8,128)(2,1)}) %all-gather.19.cloned.1.call-update) | async-done | bytes 3670032 | tf_op jit(solution)/shard_map/all_gather | solution.py:15
  649.6 2.7 copy.22
  657.1 21.9 %collective-permute-done.7 = f32[1792,128]{0,1:T(8,128)S(1)} collective-permute-done((f32[1792,128]{0,1:T(8,128)S(1)}, f32[1792,128]{0,1:T(8,128)S(1)}, u32[]{:S(2)}, u32[]{:S(2)}) %collective-permute-start.7) | collective-permute-done | bytes 917536 | tf_op jit(solution)/shard_map/ppermute | solution.py:21
  679.0 6.6 collective-permute-start.8
  691.0 116.7 %all-gather.21.cloned.1.call-done = bf16[14336,128]{0,1:T(8,128)(2,1)} async-done(((bf16[896,128]{0,1:T(8,128)(2,1)}), bf16[14336,128]{0,1:T(8,128)(2,1)}) %all-gather.21.cloned.1.call-update) | async-done | bytes 3670032 | tf_op jit(solution)/shard_map/all_gather | solution.py:15
  807.6 2.7 copy.23
  815.1 21.9 %collective-permute-done.9 = f32[1792,128]{0,1:T(8,128)S(1)} collective-permute-done((f32[1792,128]{0,1:T(8,128)S(1)}, f32[1792,128]{0,1:T(8,128)S(1)}, u32[]{:S(2)}, u32[]{:S(2)}) %collective-permute-start.9) | collective-permute-done | bytes 917536 | tf_op jit(solution)/shard_map/ppermute | solution.py:21
  837.1 6.8 collective-permute-start.10
  849.0 116.7 %all-gather.23.cloned.1.call-done = bf16[14336,128]{0,1:T(8,128)(2,1)} async-done(((bf16[896,128]{0,1:T(8,128)(2,1)}), bf16[14336,128]{0,1:T(8,128)(2,1)}) %all-gather.23.cloned.1.call-update) | async-done | bytes 3670032 | tf_op jit(solution)/shard_map/all_gather | solution.py:15
  974.6 9.4 all-to-all-start.1
  984.1 25.1 %all-to-all-done.1 = f32[32,56,128]{2,1,0:T(8,128)} async-done(((f32[32,56,128]{2,1,0:T(8,128)}), f32[32,56,128]{2,1,0:T(8,128)}, u32[]{:S(2)}, u32[]{:S(2)}) %all-to-all-start.1) | async-done | bytes 917536 | tf_op jit(solution)/shard_map/all_to_all | solution.py:67
  (96 shorter events, 85.5 us)
Async XLA Ops:
  6.5 42.1 %copy-start = (bf16[1792,896]{1,0:T(8,128)(2,1)S(1)}, bf16[1792,896]{1,0:T(8,128)(2,1)}, u32[]{:S(2)}) copy-start(bf16[1792,896]{1,0:T(8,128)(2,1)} %param.3) | copy-start | bytes 9633796
  10.2 28.2 %all-to-all-start = ((f32[32,28,128]{2,1,0:T(8,128)}), f32[32,28,128]{2,1,0:T(8,128)}, u32[]{:S(2)}, u32[]{:S(2)}) async-start(f32[32,28,128]{2,1,0:T(8,128)} %copy.11), calls=%async_computation | async-start | bytes 1048576 | tf_op jit(solution)/shard_map/all_to_all | solution.py:40
  21.5 153.8 %all-gather.13.cloned.1.call-start = ((), (), s32[]{:S(2)}) async-start(), calls=%async_computation.2 | async-start | bytes 3899392 | tf_op jit(solution)/shard_map/all_gather | solution.py:15
  43.0 4.7 collective-permute-start
  52.3 281.1 %all-gather.15.cloned.1.call-start = ((), (), s32[]{:S(2)}) async-start(), calls=%async_computation.3 | async-start | bytes 3899392 | tf_op jit(solution)/shard_map/all_gather | solution.py:15
  182.1 23.9 %collective-permute-start.1 = (f32[1792,128]{0,1:T(8,128)S(1)}, f32[1792,128]{0,1:T(8,128)S(1)}, u32[]{:S(2)}, u32[]{:S(2)}) collective-permute-start(f32[1792,128]{0,1:T(8,128)S(1)} %fusion.17), channel_id=1, source_target_pairs={{30,0},{31,1},{0,2},{1,3},{2,4},{3,5},{4,6},{5,7},{6,8},{7,9},{8,1... | collective-permute-start | bytes 2752520 | tf_op jit(solution)/shard_map/ppermute | solution.py:21
  206.0 8.7 collective-permute-start.2
  217.9 273.6 %all-gather.17.cloned.1.call-start = ((), (), s32[]{:S(2)}) async-start(), calls=%async_computation.4 | async-start | bytes 3899392 | tf_op jit(solution)/shard_map/all_gather | solution.py:15
  339.0 23.9 %collective-permute-start.3 = (f32[1792,128]{0,1:T(8,128)S(1)}, f32[1792,128]{0,1:T(8,128)S(1)}, u32[]{:S(2)}, u32[]{:S(2)}) collective-permute-start(f32[1792,128]{0,1:T(8,128)S(1)} %fusion.14), channel_id=1, source_target_pairs={{30,0},{31,1},{0,2},{1,3},{2,4},{3,5},{4,6},{5,7},{6,8},{7,9},{8,1... | collective-permute-start | bytes 2752520 | tf_op jit(solution)/shard_map/ppermute | solution.py:21
  362.9 11.2 %copy-start.6 = (f32[1792,128]{0,1:T(8,128)}, f32[1792,128]{0,1:T(8,128)S(1)}, u32[]{:S(2)}) copy-start(f32[1792,128]{0,1:T(8,128)S(1)} %collective-permute-done.3) | copy-start | bytes 2752516
  362.9 8.7 collective-permute-start.4
  374.8 274.8 %all-gather.19.cloned.1.call-start = ((), (), s32[]{:S(2)}) async-start(), calls=%async_computation.5 | async-start | bytes 3899392 | tf_op jit(solution)/shard_map/all_gather | solution.py:15
  497.1 23.9 %collective-permute-start.5 = (f32[1792,128]{0,1:T(8,128)S(1)}, f32[1792,128]{0,1:T(8,128)S(1)}, u32[]{:S(2)}, u32[]{:S(2)}) collective-permute-start(f32[1792,128]{0,1:T(8,128)S(1)} %fusion.11), channel_id=1, source_target_pairs={{30,0},{31,1},{0,2},{1,3},{2,4},{3,5},{4,6},{5,7},{6,8},{7,9},{8,1... | collective-permute-start | bytes 2752520 | tf_op jit(solution)/shard_map/ppermute | solution.py:21
  520.9 11.2 %copy-start.8 = (f32[1792,128]{0,1:T(8,128)}, f32[1792,128]{0,1:T(8,128)S(1)}, u32[]{:S(2)}) copy-start(f32[1792,128]{0,1:T(8,128)S(1)} %collective-permute-done.5) | copy-start | bytes 2752516
  520.9 8.7 collective-permute-start.6
  532.8 274.8 %all-gather.21.cloned.1.call-start = ((), (), s32[]{:S(2)}) async-start(), calls=%async_computation.6 | async-start | bytes 3899392 | tf_op jit(solution)/shard_map/all_gather | solution.py:15
  655.1 23.9 %collective-permute-start.7 = (f32[1792,128]{0,1:T(8,128)S(1)}, f32[1792,128]{0,1:T(8,128)S(1)}, u32[]{:S(2)}, u32[]{:S(2)}) collective-permute-start(f32[1792,128]{0,1:T(8,128)S(1)} %fusion.8), channel_id=1, source_target_pairs={{30,0},{31,1},{0,2},{1,3},{2,4},{3,5},{4,6},{5,7},{6,8},{7,9},{8,1... | collective-permute-start | bytes 2752520 | tf_op jit(solution)/shard_map/ppermute | solution.py:21
  679.0 11.2 %copy-start.10 = (f32[1792,128]{0,1:T(8,128)}, f32[1792,128]{0,1:T(8,128)S(1)}, u32[]{:S(2)}) copy-start(f32[1792,128]{0,1:T(8,128)S(1)} %collective-permute-done.7) | copy-start | bytes 2752516
  679.0 8.7 collective-permute-start.8
  690.9 274.8 %all-gather.23.cloned.1.call-start = ((), (), s32[]{:S(2)}) async-start(), calls=%async_computation.7 | async-start | bytes 3899392 | tf_op jit(solution)/shard_map/all_gather | solution.py:15
  813.2 23.9 %collective-permute-start.9 = (f32[1792,128]{0,1:T(8,128)S(1)}, f32[1792,128]{0,1:T(8,128)S(1)}, u32[]{:S(2)}, u32[]{:S(2)}) collective-permute-start(f32[1792,128]{0,1:T(8,128)S(1)} %fusion.5), channel_id=1, source_target_pairs={{30,0},{31,1},{0,2},{1,3},{2,4},{3,5},{4,6},{5,7},{6,8},{7,9},{8,1... | collective-permute-start | bytes 2752520 | tf_op jit(solution)/shard_map/ppermute | solution.py:21
  837.1 8.7 collective-permute-start.10
  972.2 11.9 %copy-start.12 = (s32[16]{0:T(128)S(1)}, s32[16]{0:T(128)}, u32[]{:S(2)}) copy-start(s32[16]{0:T(128)} %param.5) | copy-start | bytes 196
  974.6 34.6 %all-to-all-start.1 = ((f32[32,56,128]{2,1,0:T(8,128)}), f32[32,56,128]{2,1,0:T(8,128)}, u32[]{:S(2)}, u32[]{:S(2)}) async-start(f32[32,56,128]{2,1,0:T(8,128)} %bitcast.139), calls=%async_computation.1 | async-start | bytes 1835008 | tf_op jit(solution)/shard_map/all_to_all | solution.py:67
  (8 other events, 33.0 us)
Sparse Core Ops, SparseCore 0:
  52.5 122.8 all-gather.12
  218.0 115.3 all-gather.14
  374.9 116.5 all-gather.16
  533.0 116.5 all-gather.18
  691.0 116.5 all-gather.20
  849.1 116.5 all-gather.22
